TPU v7x, 256 devices: a whole 4x4x8 slice. The times are simulated.
256 devices in a mesh: gx: 32 (over y_lo, z, core), gy: 8 (over y_hi, x).
Axes of the slice: x: 4, y: 4 (y_hi: 2, y_lo: 2; y = y_hi * 2 + y_lo), z: 8, core: 2. Of those that a mesh axis runs over, the one named last changes fastest.
Arguments:
- populations: bfloat16 [19, 16, 512, 2048], P(None, None, 'gx', 'gy'), may hold values from 0 to 1, as said below
Outputs:
- advanced: float32 [19, 16, 512, 2048], P(None, None, 'gx', 'gy')
Inputs may be any that keep to these rules, and one draw needn't show every extreme that they name: `populations`: every population is positive.
All inputs are finite; a program needn't handle non-finite values.
Results may differ from a plain program's by a relative error of at most 0.0003.
Values sent between devices are 32-bit elements; how exact they have to be, the bound alone decides.
No kernel may reach another device: no remote copies, remote signals or barrier semaphores. Data moves between devices by JAX's collectives and lax.ppermute only.
A program may use at most 64 MiB of HBM per device.

v0:
```python
import jax
import jax.numpy as jnp
from jax import lax
from jax.experimental import pallas as pl
from jax.experimental.pallas import tpu as pltpu
from jax.sharding import PartitionSpec as P

HALO = 4
LANES = 128
STILL = (0, 3, 4, 5, 6, 15, 16, 17, 18)
RIGHT = (1, 7, 9, 11, 13)
LEFT = (2, 8, 10, 12, 14)


def pair_swap(array, axis, odd):
    size = lax.axis_size(axis)
    pairs = []
    for low in range(odd, size + odd, 2):
        a, b = low % size, (low + 1) % size
        pairs += [(a, b), (b, a)]
    return lax.ppermute(array, axis, pairs)


def iota(shape, dim):
    return lax.broadcasted_iota(jnp.int32, shape, dim)


def density(v):
    return 1.0 - jnp.exp(-v)


def loop(lo, hi, fn, unroll=4):
    count = (hi - lo) // unroll

    def group(i, c):
        for j in range(unroll):
            fn(lo + i * unroll + j)
        return c

    lax.fori_loop(0, count, group, 0)
    for left in range(lo + count * unroll, hi, 2):
        step = min(2, hi - left)
        lax.fori_loop(left, left + 1, lambda i, c: ([fn(i + j) for j in range(step)], c)[1], 0)


def moments_kernel(nz, chunks, pop_ref, rho_ref, mom_ref, o_ref, l_ref, r_ref, buf, sems):
    step = nz // chunks
    copies = []
    for c in range(chunks):
        part = pl.ds(c * step, step)
        copies.append(pltpu.make_async_copy(pop_ref.at[:, part], buf.at[:, part], sems.at[c]))
        copies[-1].start()
    rows = buf.shape[2]
    lane = iota((rows, LANES), 1)

    def plane(z, packed):
        tiles = []
        for lt in range(2):
            cols = slice(lt * LANES, (lt + 1) * LANES)

            def f(i):
                return buf[i, z, :, cols].astype(jnp.float32)

            rho, jx, jy, jz = f(0), None, None, None
            f1, f2 = f(1), f(2)
            rho, jx = rho + (f1 + f2), f1 - f2
            f1, f2 = f(3), f(4)
            rho, jy = rho + (f1 + f2), f1 - f2
            f1, f2 = f(5), f(6)
            rho, jz = rho + (f1 + f2), f1 - f2
            f1, f2 = f(7), f(8)
            d = f1 - f2
            rho, jx, jy = rho + (f1 + f2), jx + d, jy + d
            f1, f2 = f(9), f(10)
            d = f1 - f2
            rho, jx, jy = rho + (f1 + f2), jx + d, jy - d
            f1, f2 = f(11), f(12)
            d = f1 - f2
            rho, jx, jz = rho + (f1 + f2), jx + d, jz + d
            f1, f2 = f(13), f(14)
            d = f1 - f2
            rho, jx, jz = rho + (f1 + f2), jx + d, jz - d
            f1, f2 = f(15), f(16)
            d = f1 - f2
            rho, jy, jz = rho + (f1 + f2), jy + d, jz + d
            f1, f2 = f(17), f(18)
            d = f1 - f2
            rho, jy, jz = rho + (f1 + f2), jy + d, jz - d
            tiles.append((rho, jx, jy, jz))
        out = []
        group = nz - 1 - z
        shift = lax.rem(group * 8 + 4, LANES)
        for k in range(4):
            both = jnp.where(lane >= LANES - HALO, tiles[1][k], tiles[0][k])
            out.append(jnp.where(lane // 8 == group, pltpu.roll(both, shift, 1), packed[k]))
            for lt in range(2):
                v = tiles[lt][k]
                for x in range(0, rows, 8):
                    at = pl.ds(x * nz + z, 8, stride=nz)
                    if k == 0:
                        rho_ref[lt, at, :] = v[x : x + 8]
                    else:
                        mom_ref[k - 1, lt, at, :] = v[x : x + 8]
        return tuple(out)

    packed = (jnp.zeros((rows, LANES), jnp.float32),) * 4
    for c in range(chunks):
        copies[c].wait()

        def group(i, t, c=c):
            for j in range(4):
                t = plane(c * step + 4 * i + j, t)
            return t

        packed = lax.fori_loop(0, step // 4, group, packed)
    for k in range(4):
        o_ref[k] = packed[k]
    high = (lane & 7) < HALO
    for n in range(2):
        a, b = packed[2 * n : 2 * n + 2]
        l_ref[n] = jnp.where(high, pltpu.roll(b, LANES - HALO, 1), a)
        r_ref[n] = jnp.where(high, a, pltpu.roll(b, HALO, 1))


def strips_of(o, left, right):
    own = (iota(o[0].shape, 1) & 7) < HALO
    ls, rs = [], []
    for n in range(2):
        a, b = o[2 * n : 2 * n + 2]
        ls += [jnp.where(own, left[n], a), jnp.where(own, pltpu.roll(left[n], LANES - HALO, 1), b)]
        rs += [jnp.where(own, a, right[n]), jnp.where(own, b, pltpu.roll(right[n], HALO, 1))]
    return ls, rs


def pushed(p, force, momentum):
    scale = p * (1.0 / 6.0)
    return [j + scale * f for j, f in zip(momentum, force)]


def post_of(rho, momentum):
    inv = 1.0 / rho
    ux, uy, uz = [j * inv for j in momentum]
    r36 = rho * (1.0 / 36.0)
    r3 = rho * (1.0 / 12.0)
    ox, oy, oz = r3 * ux, r3 * uy, r3 * uz
    hx, hy, hz = 1.5 * ux, 1.5 * uy, 1.5 * uz
    xx, yy, zz = hx * ox, hy * oy, hz * oz
    k = r36 - (xx + yy + zz) * (1.0 / 3.0)
    kx, ky, kz = k + xx, k + yy, k + zz
    out = [12.0 * k]
    for e, o in ((kx, ox), (ky, oy), (kz, oz)):
        e2, o2 = e + e, o + o
        out += [e2 + o2, e2 - o2]
    for e, a, b, h in ((kx + yy, ox, oy, hx), (kx + zz, ox, oz, hx), (ky + zz, oy, oz, hy)):
        cross = h * b
        cross = cross + cross
        ep, em = e + cross, e - cross
        op, om = a + b, a - b
        out += [ep + op, ep - op, em + om, em - om]
    return out


def strips_of_step(strips, s_ref):
    def xp(a):
        return pltpu.roll(a, a.shape[0] - 1, 0)

    def xm(a):
        return pltpu.roll(a, 1, 0)

    def ym(a):
        return pltpu.roll(a, 1, 1)

    def yp(a):
        return pltpu.roll(a, LANES - 1, 1)

    def zm(a):
        return pltpu.roll(a, LANES - 8, 1)

    def zp(a):
        return pltpu.roll(a, 8, 1)

    def post(p, v):
        a, b = ym(p), yp(p)
        q, d = p + p + (a + b), b - a
        bb = q + (xp(p) + xm(p))
        aa = q + (zp(p) + zm(p))
        fx = xp(aa) - xm(aa)
        fy = d + d + (xp(d) + xm(d)) + (zp(d) + zm(d))
        fz = zp(bb) - zm(bb)
        return post_of(v[0], pushed(p, (fx, fy, fz), v[1:]))

    own = (iota(strips[0][0].shape, 1) & 7) < HALO
    moments, later = [], []
    for side, v in enumerate(strips):
        f = post(density(v[0]), v)
        a15, a17, a18, a16 = zm(f[15]), zp(f[17]), zm(f[18]), zp(f[16])
        sp, jp = ym(f[3] + (a15 + a17)), ym(a15 - a17)
        sn, jn = yp(f[4] + (a18 + a16)), yp(a18 - a16)
        a, b = zm(f[5]), zp(f[6])
        r0, jz0, jy0 = f[0] + (a + b) + (sp + sn), (a - b) + (jp + jn), sp - sn
        a, b, c, e = ym(f[7]), yp(f[9]), zm(f[11]), zp(f[13])
        ru, jyu, jzu = xm(f[1] + (a + b) + (c + e)), xm(a - b), xm(c - e)
        a, b, c, e = ym(f[10]), yp(f[8]), zm(f[14]), zp(f[12])
        rd, jyd, jzd = xp(f[2] + (a + b) + (c + e)), xp(a - b), xp(c - e)
        v = (r0 + (ru + rd), ru - rd, jy0 + (jyu + jyd), jz0 + (jzu + jzd))
        moments.append(v)
        p = density(v[0])
        f = post(p, v)
        if side == 0:
            later.append((p, f[3], zm(f[15]), zp(f[17]), f[7], f[10]))
        else:
            later.append((p, f[4], zp(f[16]), zm(f[18]), f[8], f[9]))
    for k in range(4):
        s_ref[k] = jnp.where(own, moments[1][k], moments[0][k])
    lane = iota(own.shape, 1) & 7
    for n in range(6):
        s_ref[4 + n] = jnp.where(lane == HALO - 1, later[0][n], pltpu.roll(later[1][n], LANES - 2, 1))


class Rows:
    def __init__(self, nz):
        self.nz = nz
        lane = iota((nz, LANES), 1)
        self.first, self.last = lane == 0, lane == LANES - 1
        self.two = lane < 2, lane >= LANES - 2

    def at(self, x):
        if isinstance(x, int):
            return pl.ds(x * self.nz, self.nz)
        return pl.ds(pl.multiple_of(x * self.nz, self.nz), self.nz)

    def of(self, ref):
        return lambda n, lt, x: ref[n, lt, self.at(x), :]

    def zp(self, v):
        return pltpu.roll(v, self.nz - 1, 0)

    def zm(self, v):
        return pltpu.roll(v, 1, 0)

    def edge(self, row, shift):
        wide = jnp.broadcast_to(row, (8, LANES))
        return jnp.concatenate(
            [pltpu.roll(wide, shift + 8 * z, 1, stride=8, stride_axis=0) for z in range(0, self.nz, 8)],
            axis=0,
        )

    def ym(self, a, h=None):
        r0, r1 = pltpu.roll(a[0], 1, 1), pltpu.roll(a[1], 1, 1)
        return r0 if h is None else jnp.where(self.first, h, r0), jnp.where(self.first, r0, r1)

    def yp(self, a, h=None):
        r0, r1 = pltpu.roll(a[0], LANES - 1, 1), pltpu.roll(a[1], LANES - 1, 1)
        return jnp.where(self.last, r1, r0), r1 if h is None else jnp.where(self.last, h, r1)

    def plane(self, x, p, w_ref, row=None):
        h = None if row is None else self.edge(row, 5)
        a, b = self.ym(p, h), self.yp(p, h)
        for lt in range(2):
            q = p[lt] + p[lt] + (a[lt] + b[lt])
            w_ref[0, lt, self.at(x), :] = p[lt]
            w_ref[1, lt, self.at(x), :] = q
            w_ref[2, lt, self.at(x), :] = q + (self.zp(p[lt]) + self.zm(p[lt]))
            w_ref[3, lt, self.at(x), :] = b[lt] - a[lt]

    def posts(self, x, lt, w, v):
        bb = w(1, lt, x) + (w(0, lt, x + 1) + w(0, lt, x - 1))
        dd = w(3, lt, x)
        fx = w(2, lt, x + 1) - w(2, lt, x - 1)
        fy = dd + dd + (self.zp(dd) + self.zm(dd)) + (w(3, lt, x + 1) + w(3, lt, x - 1))
        fz = self.zp(bb) - self.zm(bb)
        m = pushed(w(0, lt, x), (fx, fy, fz), [v(k, lt, x) for k in (1, 2, 3)])
        return post_of(v(0, lt, x), m)

    def half(self, x, other, lt, w, v):
        bb = w(1, lt, x) + w(0, lt, other)
        dd = w(3, lt, x)
        fx = w(2, lt, other) if other > x else -w(2, lt, other)
        fy = dd + dd + (self.zp(dd) + self.zm(dd)) + w(3, lt, other)
        fz = self.zp(bb) - self.zm(bb)
        return pushed(w(0, lt, x), (fx, fy, fz), [v(k, lt, x) for k in (1, 2, 3)])

    def rest(self, x, other, lt, w, v):
        p = w(0, lt, other)
        fx = w(2, lt, other) if other > x else -w(2, lt, other)
        fz = self.zp(p) - self.zm(p)
        m = pushed(w(0, lt, x), (fx, w(3, lt, other), fz), [v(k, lt, x) for k in (1, 2, 3)])
        return post_of(v(0, lt, x), m)

    def first_step(self, x, g_ref, posts):
        zp, zm = self.zp, self.zm
        part, left, right = [], [], []
        for lt in range(2):
            f = posts(lt)
            a15, a17, a18, a16 = zm(f[15]), zp(f[17]), zm(f[18]), zp(f[16])
            left.append((f[3] + (a15 + a17), a15 - a17, f[7], f[10]))
            right.append((f[4] + (a18 + a16), a18 - a16, f[9], f[8]))
            a, b = zm(f[5]), zp(f[6])
            s = [f[0] + (a + b), a - b]
            a, b = zm(f[11]), zp(f[13])
            s += [f[1] + (a + b), a - b]
            a, b = zm(f[14]), zp(f[12])
            s += [f[2] + (a + b), a - b]
            part.append(s)
        m = [self.ym((left[0][n], left[1][n])) for n in range(4)]
        q = [self.yp((right[0][n], right[1][n])) for n in range(4)]
        for lt in range(2):
            s = part[lt]

            def put(n, value):
                g_ref[n, lt, self.at(x), :] = value

            put(0, s[0] + (m[0][lt] + q[0][lt]))
            put(1, m[0][lt] - q[0][lt])
            put(2, s[1] + (m[1][lt] + q[1][lt]))
            put(3, s[2] + (m[2][lt] + q[2][lt]))
            put(4, m[2][lt] - q[2][lt])
            put(5, s[3])
            put(6, s[4] + (m[3][lt] + q[3][lt]))
            put(7, m[3][lt] - q[3][lt])
            put(8, s[5])

    def gather(self, x, g):
        out = []
        for lt in range(2):
            ru, rd = g(3, lt, x - 1), g(6, lt, x + 1)
            v = [g(0, lt, x) + (ru + rd), ru - rd]
            for k in (1, 2):
                v.append(g(k, lt, x) + (g(k + 3, lt, x - 1) + g(k + 6, lt, x + 1)))
            out.append(v)
        return out

    def patch(self, x, v, row, e_ref):
        for k in range(len(v[0])):
            h = self.edge(row(k), 4)
            v[0][k] = jnp.where(self.two[0], h, v[0][k])
            v[1][k] = jnp.where(self.two[1], h, v[1][k])
            for lt in range(2):
                e_ref[k, lt, self.at(x), :] = v[lt][k]
        return [density(v[0][0]), density(v[1][0])]

    def second_step(self, x, w, e, row, buf, shift):
        zp, zm = self.zp, self.zm
        left, right = [], []
        n, u, d = x + shift, x + shift + 1, x + shift - 1

        def put(i, row, lt, v):
            buf[row, i, :, lt * LANES : (lt + 1) * LANES] = v

        for lt in range(2):
            f = self.posts(x, lt, w, e)
            put(0, n, lt, f[0])
            put(5, n, lt, zm(f[5]))
            put(6, n, lt, zp(f[6]))
            put(1, u, lt, f[1])
            put(11, u, lt, zm(f[11]))
            put(13, u, lt, zp(f[13]))
            put(2, d, lt, f[2])
            put(12, d, lt, zp(f[12]))
            put(14, d, lt, zm(f[14]))
            left.append((f[3], zm(f[15]), zp(f[17]), f[7], f[10]))
            right.append((f[4], zp(f[16]), zm(f[18]), f[8], f[9]))
        h = [self.edge(row(5 + j), 5) for j in range(5)]
        for j, (i, to) in enumerate(((3, n), (15, n), (17, n), (7, u), (10, d))):
            v = self.ym((left[0][j], left[1][j]), h[j])
            put(i, to, 0, v[0])
            put(i, to, 1, v[1])
        for j, (i, to) in enumerate(((4, n), (16, n), (18, n), (8, d), (9, u))):
            v = self.yp((right[0][j], right[1][j]), h[j])
            put(i, to, 0, v[0])
            put(i, to, 1, v[1])


def early_kernel(nz, rows, rho_ref, mom_ref, w_ref, g_ref, e_ref, x_ref):
    r = Rows(nz)
    w, g = r.of(w_ref), r.of(g_ref)

    def v(k, lt, x):
        return rho_ref[lt, r.at(x), :] if k == 0 else mom_ref[k - 1, lt, r.at(x), :]

    def start(x):
        r.plane(x, [density(rho_ref[lt, r.at(x), :]) for lt in range(2)], w_ref)

    def first(x):
        r.first_step(x, g_ref, lambda lt: r.posts(x, lt, w, v))

    def middle(x):
        v = r.gather(x, g)
        for lt in range(2):
            for k in range(4):
                e_ref[k, lt, r.at(x), :] = v[lt][k]

    loop(0, rows, start, 16)
    for side, x, other in ((0, 0, 1), (1, rows - 1, rows - 2)):
        for lt in range(2):
            x_ref[side, r.at(8 + lt), :] = v(0, lt, x)
            for k, j in enumerate(r.half(x, other, lt, w, v)):
                x_ref[side, r.at(10 + 2 * k + lt), :] = j
    loop(1, rows - 1, first, 14)
    loop(2, rows - 2, middle, 12)
    for side, base, x, other in ((0, 6, 1, 2), (1, 3, rows - 2, rows - 3)):
        for lt in range(2):
            x_ref[side, r.at(lt), :] = g(0, lt, x) + g(base, lt, other)
            for k in range(3):
                x_ref[side, r.at(2 + 2 * k + lt), :] = g(base + k, lt, x)


def inner_kernel(nz, rows, e_in, o_ref, l_ref, r_ref, buf, e_ref, w_ref, s_ref):
    r = Rows(nz)
    strips_of_step(
        strips_of(
            [o_ref[k] for k in range(4)], [l_ref[k] for k in range(2)], [r_ref[k] for k in range(2)]
        ),
        s_ref,
    )

    def row(x):
        return lambda n: s_ref[n, pl.ds(x, 1), :]

    def middle(x):
        v = [[e_in[k, lt, r.at(x), :] for k in range(4)] for lt in range(2)]
        p = r.patch(x, v, row(x), e_ref)
        r.plane(x, p, w_ref, row(x)(4))

    def second(x):
        r.second_step(x, r.of(w_ref), r.of(e_ref), row(x), buf, -2)

    loop(2, rows - 2, middle, 12)
    loop(3, rows - 3, second, 10)


def outer_kernel(nz, rows, x_ref, o_ref, l_ref, r_ref, hl_ref, hr_ref, w0_in, g_in, e_in, w1_in, buf_in,
                 out_ref, w0_ref, g_ref, e_ref, w1_ref, s_ref, buf, sems):
    r = Rows(nz)

    def send(source, x):
        return pltpu.make_async_copy(source, out_ref.at[:, :, x, :], sems.at[x])

    inside = [send(buf_in.at[x - 2], x) for x in range(HALO, rows - HALO)]
    for copy in inside[:2]:
        copy.start()
    low = iota((8, LANES), 0) < HALO

    def with_halo(local, t, upper):
        at = pl.ds(16 * nz + 8 * t, 8)
        hl, hr = hl_ref[at, :], hr_ref[at, :]
        if upper:
            tile = jnp.where(low, pltpu.roll(hr, HALO, 0), hl)
        else:
            tile = jnp.where(low, hr, pltpu.roll(hl, HALO, 0))
        return jnp.concatenate([local, tile], axis=0)

    strips_of_step(
        strips_of(
            [with_halo(o_ref[k], 2 + k % 2, k >= 2) for k in range(4)],
            [with_halo(l_ref[k], k, False) for k in range(2)],
            [with_halo(r_ref[k], k, True) for k in range(2)],
        ),
        s_ref,
    )
    ring = rows + 2 * HALO

    def x_of(l):
        return l - HALO if l < 10 else l - 16 + rows

    def row(l):
        return lambda n: s_ref[n, pl.ds(x_of(l) % ring, 1), :]

    def either(ref, ref_in, inside):
        def get(n, lt, l):
            if inside <= x_of(l) < rows - inside:
                return ref_in[n, lt, r.at(x_of(l)), :]
            return ref[n, lt, r.at(l), :]

        return get

    def edge(l):
        ref = {3: hl_ref, 4: x_ref.at[0], 15: x_ref.at[1], 16: hr_ref}[l]
        return lambda k, lt, x: ref[r.at(8 + 2 * k + lt), :]

    w0 = either(w0_ref, w0_in, 0)
    for l in (3, 16):
        r.plane(l, [density(edge(l)(0, lt, l)) for lt in range(2)], w0_ref)
    for l, other in ((3, 4), (4, 3), (15, 16), (16, 15)):
        r.first_step(l, g_ref, lambda lt: r.rest(l, other, lt, w0, edge(l)))

    for copy in inside[2:]:
        copy.start()
    own = either(g_ref, g_in, 1)

    def g(n, lt, l):
        if l == 2 or l == 17:
            ref = hl_ref if l == 2 else hr_ref
            return ref[r.at(2 + 2 * (n % 3) + lt), :]
        return own(n, lt, l)

    for l, ref, n, near in ((2, hl_ref, 6, 3), (17, hr_ref, 3, 16)):
        v = [[ref[r.at(lt), :] + g_ref[n, lt, r.at(near), :]] for lt in range(2)]
        r.plane(l, r.patch(l, v, row(l), e_ref), w1_ref, row(l)(4))
    for l in (3, 4, 5, 14, 15, 16):
        p = r.patch(l, r.gather(l, g), row(l), e_ref)
        r.plane(l, p, w1_ref, row(l)(4))

    for l, x, indices in (
        (6, 2, LEFT),
        (7, 3, STILL + LEFT),
        (12, rows - 4, STILL + RIGHT),
        (13, rows - 3, RIGHT),
    ):
        for i in indices:
            buf[l, i] = buf_in[x - 2, i]

    w1, e = either(w1_ref, w1_in, 2), either(e_ref, e_in, 2)
    edges = []
    for side in range(2):
        for n in (3, 2, 1, 0):
            l, x = ((n + 3, n), (16 - n, rows - 1 - n))[side]
            r.second_step(l, w1, e, row(l), buf, 0)
            edges.append(send(buf.at[l + 1 if x == n else l - 1], x))
            edges[-1].start()
    for copy in inside + edges:
        copy.wait()


def body(populations):
    _, nz, rows, columns = populations.shape
    f32 = jnp.float32
    even_x = (lax.axis_index("gx") & 1) == 0
    even_y = (lax.axis_index("gy") & 1) == 0
    vmem = pl.BlockSpec(memory_space=pltpu.VMEM)
    hbm = pl.BlockSpec(memory_space=pltpu.HBM)
    chunks = 4
    params = pltpu.CompilerParams(vmem_limit_bytes=40 * 1024 * 1024)

    def shape(*dims):
        return jax.ShapeDtypeStruct(dims, f32)

    def field(n, count):
        return (n, 2, count * nz, LANES)

    def moments(*refs):
        moments_kernel(nz, chunks, *refs)

    rho, mom, o, to_left, to_right = pl.pallas_call(
        moments,
        out_shape=(
            shape(2, rows * nz, LANES), shape(*field(3, rows)), shape(4, rows, LANES),
            shape(2, rows, LANES), shape(2, rows, LANES),
        ),
        in_specs=[hbm],
        out_specs=(vmem, vmem, vmem, vmem, vmem),
        scratch_shapes=[
            pltpu.VMEM(populations.shape, populations.dtype),
            pltpu.SemaphoreType.DMA((chunks,)),
        ],
        compiler_params=pltpu.CompilerParams(vmem_limit_bytes=50 * 1024 * 1024),
        name="moments",
    )(pltpu.with_memory_space_constraint(populations, pltpu.HBM))

    def both(array_odd, array_even, axis):
        odd = pair_swap(array_odd, axis, 1)
        even = pair_swap(array_even, axis, 0)
        odd = lax.optimization_barrier(-odd)
        return -odd, even

    ob, oa = both(
        jnp.where(even_y, to_left, to_right), jnp.where(even_y, to_right, to_left), "gy"
    )

    left, right = jnp.where(even_y, ob, oa), jnp.where(even_y, oa, ob)

    def early(*refs):
        early_kernel(nz, rows, *refs)

    w0, g, e0, edges = pl.pallas_call(
        early,
        out_shape=(
            shape(*field(4, rows)), shape(*field(9, rows)), shape(*field(4, rows)),
            shape(2, 16 * nz, LANES),
        ),
        in_specs=[vmem, vmem],
        out_specs=(vmem, vmem, vmem, vmem),
        compiler_params=params,
        cost_estimate=pl.CostEstimate(flops=10_000_000, bytes_accessed=2_500_000, transcendentals=0),
        name="early",
    )(rho, mom)

    left, right, edges, e0 = lax.optimization_barrier((left, right, edges, e0))

    def edge(low):
        c = slice(0, HALO) if low else slice(rows - HALO, rows)
        return jnp.concatenate([
            edges[0 if low else 1],
            jnp.concatenate([left[:, c], right[:, c]], axis=1).reshape(-1, LANES),
            jnp.concatenate([o[:2, c], o[2:, c]], axis=1).reshape(-1, LANES),
        ])

    low, high = edge(True), edge(False)
    hb, ha = both(jnp.where(even_x, low, high), jnp.where(even_x, high, low), "gx")

    def inner(*refs):
        inner_kernel(nz, rows, *refs)

    buf, e, w1 = pl.pallas_call(
        inner,
        out_shape=(
            shape(rows - HALO, 19, nz, columns), shape(*field(4, rows)), shape(*field(4, rows)),
        ),
        in_specs=[vmem] * 4,
        out_specs=(vmem, vmem, vmem),
        scratch_shapes=[pltpu.VMEM((10, rows, LANES), f32)],
        compiler_params=params,
        cost_estimate=pl.CostEstimate(flops=10_000_000, bytes_accessed=2_500_000, transcendentals=0),
        name="inner",
    )(e0, o, left, right)
    hl, hr = jnp.where(even_x, hb, ha), jnp.where(even_x, ha, hb)

    def outer(*refs):
        outer_kernel(nz, rows, *refs)

    ring = rows + 2 * HALO
    return pl.pallas_call(
        outer,
        out_shape=shape(*populations.shape),
        in_specs=[vmem] * 11,
        out_specs=hbm,
        scratch_shapes=[
            pltpu.VMEM(field(4, 20), f32),
            pltpu.VMEM(field(9, 20), f32),
            pltpu.VMEM(field(4, 20), f32),
            pltpu.VMEM(field(4, 20), f32),
            pltpu.VMEM((10, ring, LANES), f32),
            pltpu.VMEM((20, 19, nz, columns), f32),
            pltpu.SemaphoreType.DMA((rows,)),
        ],
        compiler_params=params,
        name="outer",
    )(edges, o, left, right, hl, hr, w0, g, e, w1, buf)


def solution(mesh):
    return jax.shard_map(
        body,
        mesh=mesh,
        in_specs=(P(None, None, "gx", "gy"),),
        out_specs=P(None, None, "gx", "gy"),
        check_vma=False,
    )
```

profile of v0, /device:TPU:1, one launch (start us, length us, event | category | flops | bytes accessed | tf_op | source)
XLA Modules:
  0.0 22.0 jit_solution(14762082571017946900)
XLA Ops:
  0.0 2.2 %moments.1 = (f32[2,256,128]{2,1,0:T(8,128)S(1)}, f32[3,2,256,128]{3,2,1,0:T(8,128)S(1)}, f32[4,16,128]{2,1,0:T(8,128)S(1)}, f32[2,16,128]{2,1,0:T(8,128)S(1)}, f32[2,16,128]{2,1,0:T(8,128)S(1)}) custom-call(bf16[19,16,16,256]{3,2,1,0:T(8,128)(2,1)} %refs_0_.1), custom_call_target="tpu_custom_call" | custom-call | tf_op jit(solution)/shard_map/moments/pallas_call | solution.py:544
  2.2 6.0 %collective-permute-start = (f32[2,16,128]{2,1,0:T(8,128)S(1)}, f32[2,16,128]{2,1,0:T(8,128)S(1)}, u32[]{:S(2)}, u32[]{:S(2)}) collective-permute-start(f32[2,16,128]{2,1,0:T(8,128)S(1)} %get-tuple-element.49), channel_id=1, source_target_pairs={{1,2},{2,1},{3,4},{4,3},{5,6},{6,5},{7,0},{0,7},{9,10},{10,9},{11,... | collective-permute-start | bytes 49160 | tf_op jit(solution)/shard_map/ppermute | solution.py:21
  8.3 0.0 collective-permute-start.1
  8.3 1.4 %early.1 = (f32[4,2,256,128]{3,2,1,0:T(8,128)S(1)}, f32[9,2,256,128]{3,2,1,0:T(8,128)S(1)}, f32[4,2,256,128]{3,2,1,0:T(8,128)S(1)}, f32[2,256,128]{2,1,0:T(8,128)S(1)}) custom-call(f32[2,256,128]{2,1,0:T(8,128)S(1)} %get-tuple-element.23.refs_0_, f32[3,2,256,128]{3,2,1,0:T(8,128)S(1)} %get-tuple-element.24.refs_1_), custom_call_target="tpu_custom_call" | custom-call | flops 10000000 | bytes 2500000 | tf_op jit(solution)/shard_map/early/pallas_call | solution.py:575
  9.7 0.0 collective-permute-done
  9.7 1.4 %collective-permute-done.1 = f32[2,16,128]{2,1,0:T(8,128)S(1)} collective-permute-done((f32[2,16,128]{2,1,0:T(8,128)S(1)}, f32[2,16,128]{2,1,0:T(8,128)S(1)}, u32[]{:S(2)}, u32[]{:S(2)}) %collective-permute-start.1) | collective-permute-done | bytes 16416 | tf_op jit(solution)/shard_map/ppermute | solution.py:21
  11.2 3.4 %collective-permute-start.2 = (f32[288,128]{1,0:T(8,128)S(1)}, f32[288,128]{1,0:T(8,128)S(1)}, u32[]{:S(2)}, u32[]{:S(2)}) collective-permute-start(f32[288,128]{1,0:T(8,128)S(1)} %get-tuple-element.39), channel_id=1, source_target_pairs={{8,16},{16,8},{24,32},{32,24},{40,48},{48,40},{56,64},{64,56},{72,... | collective-permute-start | bytes 442376 | tf_op jit(solution)/shard_map/ppermute | solution.py:21
  14.7 2.8 %collective-permute-start.3 = (f32[288,128]{1,0:T(8,128)S(1)}, f32[288,128]{1,0:T(8,128)S(1)}, u32[]{:S(2)}, u32[]{:S(2)}) collective-permute-start(f32[288,128]{1,0:T(8,128)S(1)} %get-tuple-element.40), channel_id=1, source_target_pairs={{0,8},{8,0},{16,24},{24,16},{32,40},{40,32},{48,56},{56,48},{64,72... | collective-permute-start | bytes 442376 | tf_op jit(solution)/shard_map/ppermute | solution.py:21
  17.4 1.5 %inner.1 = (f32[12,19,16,256]{3,2,1,0:T(8,128)S(1)}, f32[4,2,256,128]{3,2,1,0:T(8,128)S(1)}, f32[4,2,256,128]{3,2,1,0:T(8,128)S(1)}) custom-call(f32[4,2,256,128]{3,2,1,0:T(8,128)S(1)} %get-tuple-element.33.refs_0_, f32[4,16,128]{2,1,0:T(8,128)S(1)} %get-tuple-element.28.refs_1_, f32[2,16,128]{2,1,0:T(8,128)S(1)} %get-tuple-element.29.refs_2_, ...), custom_call_target="tpu_custom_call" | custom-call | flops 10000000 | bytes 2500000 | tf_op jit(solution)/shard_map/inner/pallas_call | solution.py:604
  18.9 0.0 collective-permute-done.2
  18.9 0.0 collective-permute-done.3
  19.0 3.0 %outer.1 = f32[19,16,16,256]{3,2,1,0:T(8,128)} custom-call(f32[2,256,128]{2,1,0:T(8,128)S(1)} %get-tuple-element.27.refs_0_, f32[4,16,128]{2,1,0:T(8,128)S(1)} %get-tuple-element.28.refs_1_, f32[2,16,128]{2,1,0:T(8,128)S(1)} %get-tuple-element.29.refs_2_, f32[2,16,128]{2,1,0:T(8,128)S(1)} %get-tuple-element.30.refs_3_, ...), custom_call_target="tpu_custom_call" | custom-call | tf_op jit(solution)/shard_map/outer/pallas_call | solution.py:622
  (12 shorter events, 0.1 us)
Async XLA Ops:
  2.2 7.4 %collective-permute-start = (f32[2,16,128]{2,1,0:T(8,128)S(1)}, f32[2,16,128]{2,1,0:T(8,128)S(1)}, u32[]{:S(2)}, u32[]{:S(2)}) collective-permute-start(f32[2,16,128]{2,1,0:T(8,128)S(1)} %get-tuple-element.49), channel_id=1, source_target_pairs={{1,2},{2,1},{3,4},{4,3},{5,6},{6,5},{7,0},{0,7},{9,10},{10,9},{11,... | collective-permute-start | bytes 49160 | tf_op jit(solution)/shard_map/ppermute | solution.py:21
  8.3 2.9 %collective-permute-start.1 = (f32[2,16,128]{2,1,0:T(8,128)S(1)}, f32[2,16,128]{2,1,0:T(8,128)S(1)}, u32[]{:S(2)}, u32[]{:S(2)}) collective-permute-start(f32[2,16,128]{2,1,0:T(8,128)S(1)} %get-tuple-element.50), channel_id=1, source_target_pairs={{0,1},{1,0},{2,3},{3,2},{4,5},{5,4},{6,7},{7,6},{8,9},{9,8},{10,11... | collective-permute-start | bytes 49160 | tf_op jit(solution)/shard_map/ppermute | solution.py:21
  11.2 7.7 %collective-permute-start.2 = (f32[288,128]{1,0:T(8,128)S(1)}, f32[288,128]{1,0:T(8,128)S(1)}, u32[]{:S(2)}, u32[]{:S(2)}) collective-permute-start(f32[288,128]{1,0:T(8,128)S(1)} %get-tuple-element.39), channel_id=1, source_target_pairs={{8,16},{16,8},{24,32},{32,24},{40,48},{48,40},{56,64},{64,56},{72,... | collective-permute-start | bytes 442376 | tf_op jit(solution)/shard_map/ppermute | solution.py:21
  14.7 4.3 %collective-permute-start.3 = (f32[288,128]{1,0:T(8,128)S(1)}, f32[288,128]{1,0:T(8,128)S(1)}, u32[]{:S(2)}, u32[]{:S(2)}) collective-permute-start(f32[288,128]{1,0:T(8,128)S(1)} %get-tuple-element.40), channel_id=1, source_target_pairs={{0,8},{8,0},{16,24},{24,16},{32,40},{40,32},{48,56},{56,48},{64,72... | collective-permute-start | bytes 442376 | tf_op jit(solution)/shard_map/ppermute | solution.py:21
where the time goes:
time: 22.1 us; the launch traced here: 22 us
  starting transfers between devices  12.2 us (55%)
  Pallas kernels  8.05 us (36%)
  waiting for transfers between devices  1.46 us (7%)
    ppermute x4, starting transfers between devices, pair_swap(): return lax.ppermute(array, axis, pairs)  12.2 us
    pallas_call x1, Pallas kernels, body(): pl.pallas_call(outer, out_shape=shape(*populations.shape), in_specs=[vmem...  2.99 us
    pallas_call x1, Pallas kernels, body(): pl.pallas_call(moments, out_shape=(shape(2, rows * nz, LANES), shape(*fie...  2.2 us
    pallas_call x1, Pallas kernels, body(): pl.pallas_call(inner, out_shape=(shape(rows - HALO, 19, nz, columns), sha...  1.49 us
    ppermute x4, waiting for transfers between devices, pair_swap(): return lax.ppermute(array, axis, pairs)  1.46 us
    pallas_call x1, Pallas kernels, body(): pl.pallas_call(early, out_shape=(shape(*field(4, rows)), shape(*field(9,...  1.37 us
  transfers between devices with their start and end apart: 4, of which 1 were waited for; matrix products, arithmetic and copies ran while one was open for 0% of the time, Pallas kernels for 13%

commit v1 on v0

--- a/solution.py
+++ b/solution.py
@@ -481,7 +481,7 @@
     w0 = either(w0_ref, w0_in, 0)
     for l in (3, 16):
         r.plane(l, [density(edge(l)(0, lt, l)) for lt in range(2)], w0_ref)
-    for l, other in ((3, 4), (4, 3), (15, 16), (16, 15)):
+    for l, other in ((4, 3), (15, 16), (3, 4), (16, 15)):
         r.first_step(l, g_ref, lambda lt: r.rest(l, other, lt, w0, edge(l)))
 
     for copy in inside[2:]:
@@ -494,13 +494,13 @@
             return ref[r.at(2 + 2 * (n % 3) + lt), :]
         return own(n, lt, l)
 
+    for l in (5, 14, 4, 15, 3, 16):
+        p = r.patch(l, r.gather(l, g), row(l), e_ref)
+        r.plane(l, p, w1_ref, row(l)(4))
+
     for l, ref, n, near in ((2, hl_ref, 6, 3), (17, hr_ref, 3, 16)):
         v = [[ref[r.at(lt), :] + g_ref[n, lt, r.at(near), :]] for lt in range(2)]
         r.plane(l, r.patch(l, v, row(l), e_ref), w1_ref, row(l)(4))
-    for l in (3, 4, 5, 14, 15, 16):
-        p = r.patch(l, r.gather(l, g), row(l), e_ref)
-        r.plane(l, p, w1_ref, row(l)(4))
-
     for l, x, indices in (
         (6, 2, LEFT),
         (7, 3, STILL + LEFT),

time: 22.1 us -> 22 us (level)
  no operation moved by 1% of the time
where the time goes in v1:
time: 22 us
  starting transfers between devices  12.2 us (55%)
  Pallas kernels  8.03 us (36%)
  waiting for transfers between devices  1.46 us (7%)
    ppermute x4, starting transfers between devices, pair_swap(): return lax.ppermute(array, axis, pairs)  12.2 us
    pallas_call x1, Pallas kernels, body(): pl.pallas_call(outer, out_shape=shape(*populations.shape), in_specs=[vmem...  2.97 us
    pallas_call x1, Pallas kernels, body(): pl.pallas_call(moments, out_shape=(shape(2, rows * nz, LANES), shape(*fie...  2.2 us
    pallas_call x1, Pallas kernels, body(): pl.pallas_call(inner, out_shape=(shape(rows - HALO, 19, nz, columns), sha...  1.49 us
    ppermute x4, waiting for transfers between devices, pair_swap(): return lax.ppermute(array, axis, pairs)  1.46 us
    pallas_call x1, Pallas kernels, body(): pl.pallas_call(early, out_shape=(shape(*field(4, rows)), shape(*field(9,...  1.37 us
  transfers between devices with their start and end apart: 4, of which 1 were waited for; matrix products, arithmetic and copies ran while one was open for 0% of the time, Pallas kernels for 13%

profile of v1, /device:TPU:1, one launch (start us, length us, event | category | flops | bytes accessed | tf_op | source)
XLA Modules:
  0.0 22.0 jit_solution(7169430459071162360)
XLA Ops:
  0.0 2.2 %moments.1 = (f32[2,256,128]{2,1,0:T(8,128)S(1)}, f32[3,2,256,128]{3,2,1,0:T(8,128)S(1)}, f32[4,16,128]{2,1,0:T(8,128)S(1)}, f32[2,16,128]{2,1,0:T(8,128)S(1)}, f32[2,16,128]{2,1,0:T(8,128)S(1)}) custom-call(bf16[19,16,16,256]{3,2,1,0:T(8,128)(2,1)} %refs_0_.1), custom_call_target="tpu_custom_call" | custom-call | tf_op jit(solution)/shard_map/moments/pallas_call | solution.py:544
  2.2 6.0 %collective-permute-start = (f32[2,16,128]{2,1,0:T(8,128)S(1)}, f32[2,16,128]{2,1,0:T(8,128)S(1)}, u32[]{:S(2)}, u32[]{:S(2)}) collective-permute-start(f32[2,16,128]{2,1,0:T(8,128)S(1)} %get-tuple-element.49), channel_id=1, source_target_pairs={{1,2},{2,1},{3,4},{4,3},{5,6},{6,5},{7,0},{0,7},{9,10},{10,9},{11,... | collective-permute-start | bytes 49160 | tf_op jit(solution)/shard_map/ppermute | solution.py:21
  8.3 0.0 collective-permute-start.1
  8.3 1.4 %early.1 = (f32[4,2,256,128]{3,2,1,0:T(8,128)S(1)}, f32[9,2,256,128]{3,2,1,0:T(8,128)S(1)}, f32[4,2,256,128]{3,2,1,0:T(8,128)S(1)}, f32[2,256,128]{2,1,0:T(8,128)S(1)}) custom-call(f32[2,256,128]{2,1,0:T(8,128)S(1)} %get-tuple-element.23.refs_0_, f32[3,2,256,128]{3,2,1,0:T(8,128)S(1)} %get-tuple-element.24.refs_1_), custom_call_target="tpu_custom_call" | custom-call | flops 10000000 | bytes 2500000 | tf_op jit(solution)/shard_map/early/pallas_call | solution.py:575
  9.7 0.0 collective-permute-done
  9.7 1.4 %collective-permute-done.1 = f32[2,16,128]{2,1,0:T(8,128)S(1)} collective-permute-done((f32[2,16,128]{2,1,0:T(8,128)S(1)}, f32[2,16,128]{2,1,0:T(8,128)S(1)}, u32[]{:S(2)}, u32[]{:S(2)}) %collective-permute-start.1) | collective-permute-done | bytes 16416 | tf_op jit(solution)/shard_map/ppermute | solution.py:21
  11.2 3.4 %collective-permute-start.2 = (f32[288,128]{1,0:T(8,128)S(1)}, f32[288,128]{1,0:T(8,128)S(1)}, u32[]{:S(2)}, u32[]{:S(2)}) collective-permute-start(f32[288,128]{1,0:T(8,128)S(1)} %get-tuple-element.39), channel_id=1, source_target_pairs={{8,16},{16,8},{24,32},{32,24},{40,48},{48,40},{56,64},{64,56},{72,... | collective-permute-start | bytes 442376 | tf_op jit(solution)/shard_map/ppermute | solution.py:21
  14.7 2.8 %collective-permute-start.3 = (f32[288,128]{1,0:T(8,128)S(1)}, f32[288,128]{1,0:T(8,128)S(1)}, u32[]{:S(2)}, u32[]{:S(2)}) collective-permute-start(f32[288,128]{1,0:T(8,128)S(1)} %get-tuple-element.40), channel_id=1, source_target_pairs={{0,8},{8,0},{16,24},{24,16},{32,40},{40,32},{48,56},{56,48},{64,72... | collective-permute-start | bytes 442376 | tf_op jit(solution)/shard_map/ppermute | solution.py:21
  17.4 1.5 %inner.1 = (f32[12,19,16,256]{3,2,1,0:T(8,128)S(1)}, f32[4,2,256,128]{3,2,1,0:T(8,128)S(1)}, f32[4,2,256,128]{3,2,1,0:T(8,128)S(1)}) custom-call(f32[4,2,256,128]{3,2,1,0:T(8,128)S(1)} %get-tuple-element.33.refs_0_, f32[4,16,128]{2,1,0:T(8,128)S(1)} %get-tuple-element.28.refs_1_, f32[2,16,128]{2,1,0:T(8,128)S(1)} %get-tuple-element.29.refs_2_, ...), custom_call_target="tpu_custom_call" | custom-call | flops 10000000 | bytes 2500000 | tf_op jit(solution)/shard_map/inner/pallas_call | solution.py:604
  18.9 0.0 collective-permute-done.2
  18.9 0.0 collective-permute-done.3
  19.0 3.0 %outer.1 = f32[19,16,16,256]{3,2,1,0:T(8,128)} custom-call(f32[2,256,128]{2,1,0:T(8,128)S(1)} %get-tuple-element.27.refs_0_, f32[4,16,128]{2,1,0:T(8,128)S(1)} %get-tuple-element.28.refs_1_, f32[2,16,128]{2,1,0:T(8,128)S(1)} %get-tuple-element.29.refs_2_, f32[2,16,128]{2,1,0:T(8,128)S(1)} %get-tuple-element.30.refs_3_, ...), custom_call_target="tpu_custom_call" | custom-call | tf_op jit(solution)/shard_map/outer/pallas_call | solution.py:622
  (12 shorter events, 0.1 us)
Async XLA Ops:
  2.2 7.4 %collective-permute-start = (f32[2,16,128]{2,1,0:T(8,128)S(1)}, f32[2,16,128]{2,1,0:T(8,128)S(1)}, u32[]{:S(2)}, u32[]{:S(2)}) collective-permute-start(f32[2,16,128]{2,1,0:T(8,128)S(1)} %get-tuple-element.49), channel_id=1, source_target_pairs={{1,2},{2,1},{3,4},{4,3},{5,6},{6,5},{7,0},{0,7},{9,10},{10,9},{11,... | collective-permute-start | bytes 49160 | tf_op jit(solution)/shard_map/ppermute | solution.py:21
  8.3 2.9 %collective-permute-start.1 = (f32[2,16,128]{2,1,0:T(8,128)S(1)}, f32[2,16,128]{2,1,0:T(8,128)S(1)}, u32[]{:S(2)}, u32[]{:S(2)}) collective-permute-start(f32[2,16,128]{2,1,0:T(8,128)S(1)} %get-tuple-element.50), channel_id=1, source_target_pairs={{0,1},{1,0},{2,3},{3,2},{4,5},{5,4},{6,7},{7,6},{8,9},{9,8},{10,11... | collective-permute-start | bytes 49160 | tf_op jit(solution)/shard_map/ppermute | solution.py:21
  11.2 7.7 %collective-permute-start.2 = (f32[288,128]{1,0:T(8,128)S(1)}, f32[288,128]{1,0:T(8,128)S(1)}, u32[]{:S(2)}, u32[]{:S(2)}) collective-permute-start(f32[288,128]{1,0:T(8,128)S(1)} %get-tuple-element.39), channel_id=1, source_target_pairs={{8,16},{16,8},{24,32},{32,24},{40,48},{48,40},{56,64},{64,56},{72,... | collective-permute-start | bytes 442376 | tf_op jit(solution)/shard_map/ppermute | solution.py:21
  14.7 4.3 %collective-permute-start.3 = (f32[288,128]{1,0:T(8,128)S(1)}, f32[288,128]{1,0:T(8,128)S(1)}, u32[]{:S(2)}, u32[]{:S(2)}) collective-permute-start(f32[288,128]{1,0:T(8,128)S(1)} %get-tuple-element.40), channel_id=1, source_target_pairs={{0,8},{8,0},{16,24},{24,16},{32,40},{40,32},{48,56},{56,48},{64,72... | collective-permute-start | bytes 442376 | tf_op jit(solution)/shard_map/ppermute | solution.py:21
